TPU v7x, 512 devices: a whole 4x4x16 slice. The times are simulated.
512 devices in a mesh: seq: 64 (over x, z_lo, core), head: 8 (over y, z_hi).
Axes of the slice: x: 4, y: 4, z: 16 (z_hi: 2, z_lo: 8; z = z_hi * 8 + z_lo), core: 2. Of those that a mesh axis runs over, the one named last changes fastest.
Arguments:
- queries: bfloat16 [16384, 8192], P(('seq', 'head')), may hold values from -8 to 8
- cache_keys: bfloat16 [4096, 1024], P('seq', 'head'), may hold values from -4 to 4
- cache_values: bfloat16 [4096, 1024], P('seq', 'head'), may hold values from -4 to 4
- slab_keys: bfloat16 [16384, 1024], P('seq', 'head'), may hold values from -4 to 4
- slab_values: bfloat16 [16384, 1024], P('seq', 'head'), may hold values from -4 to 4
- block_lists: int32 [64, 256, 24], P('head', 'seq'), may hold values from 0 to 63, as said below
Outputs:
- attended: bfloat16 [16384, 8192], P(('seq', 'head'))
Inputs may be any that keep to these rules, and one draw needn't show every extreme that they name: `block_lists`: for each head and query block the 24 entries are distinct. Entries 0 to 11 are the head's vertical blocks, the same for all its query blocks, all below 32, the first one 0. Entry 12 + j of query block q is 32 + (o_j + q) mod (32) for the head's own distinct offsets o_j.
All inputs are finite; a program needn't handle non-finite values.
Results may differ from a plain program's by a relative error of at most 0.0049.
Values may be sent and summed in bfloat16 or wider, within the bound.
No kernel may reach another device: no remote copies, remote signals or barrier semaphores. Data moves between devices by JAX's collectives and lax.ppermute only.
A program may use at most 64 MiB of HBM per device.

v0:
```python
import jax
import jax.numpy as jnp
from jax import lax
from jax.sharding import PartitionSpec as P

DH = 128
BLOCK = 64
WIN = 4


def softmax_weights(logit_matrix, allowed):
    masked = jnp.where(allowed, logit_matrix, -jnp.inf)
    highest = jnp.max(masked, axis=-1, keepdims=True)
    raised = jnp.exp(masked - highest)
    return (raised / jnp.sum(raised, axis=-1, keepdims=True)).astype(jnp.bfloat16)


def per_device(queries, cache_keys, cache_values, slab_keys, slab_values, block_lists):
    head_count = block_lists.shape[0]
    blocks_here = block_lists.shape[1]
    listed = block_lists.shape[2]
    kv_count = cache_keys.shape[1] // DH
    group_size = head_count // kv_count
    seq_position = lax.axis_index("seq")
    offsets = jnp.arange(WIN, dtype=jnp.int32)
    query_blocks = seq_position * blocks_here + jnp.arange(blocks_here, dtype=jnp.int32)
    slab_valid = query_blocks[:, None] - offsets[None, :] >= 0
    arrived = lax.all_to_all(queries, "head", split_axis=1, concat_axis=0, tiled=True)
    gathered_keys = lax.all_gather(cache_keys, "seq", axis=0, tiled=True)
    gathered_values = lax.all_gather(cache_values, "seq", axis=0, tiled=True)
    source_keys = lax.all_gather(slab_keys, "seq", axis=0, tiled=True)
    source_values = lax.all_gather(slab_values, "seq", axis=0, tiled=True)
    fetch_slab_index = jnp.maximum(query_blocks[:, None] - offsets[None, :], 0)
    fetched = (gathered_keys, gathered_values, source_keys, source_values, fetch_slab_index)
    gathered_keys, gathered_values, source_keys, source_values, slab_index = fetched

    def as_blocks(array):
        return array.reshape(array.shape[0] // BLOCK, BLOCK, kv_count, DH).transpose(2, 0, 1, 3)

    cache_key_blocks = as_blocks(gathered_keys)
    cache_value_blocks = as_blocks(gathered_values)
    slab_key_blocks = as_blocks(source_keys)
    slab_value_blocks = as_blocks(source_values)
    rows_in_block = jnp.arange(BLOCK, dtype=jnp.int32)
    causal = rows_in_block[None, :] <= rows_in_block[:, None]
    slab_mask = slab_valid[:, None, :, None] & (
        (offsets[None, None, :, None] > 0) | causal[None, :, None, :]
    )
    slab_mask = slab_mask.reshape(blocks_here, BLOCK, WIN * BLOCK)
    full_mask = jnp.concatenate(
        [jnp.ones((blocks_here, BLOCK, listed * BLOCK), dtype=bool), slab_mask], axis=2
    )
    query_heads = arrived.reshape(blocks_here, BLOCK, head_count, DH).transpose(2, 0, 1, 3)
    score_scale = DH ** (-0.5)

    def attend(query_tile_rows, lists, head_number):
        kv_number = head_number // group_size
        cache_k = lax.dynamic_index_in_dim(cache_key_blocks, kv_number, 0, keepdims=False)
        cache_v = lax.dynamic_index_in_dim(cache_value_blocks, kv_number, 0, keepdims=False)
        slab_k = lax.dynamic_index_in_dim(slab_key_blocks, kv_number, 0, keepdims=False)
        slab_v = lax.dynamic_index_in_dim(slab_value_blocks, kv_number, 0, keepdims=False)
        selected_key_rows = jnp.concatenate(
            [
                jnp.take(cache_k, lists, axis=0).reshape(blocks_here, listed * BLOCK, DH),
                jnp.take(slab_k, slab_index, axis=0).reshape(blocks_here, WIN * BLOCK, DH),
            ],
            axis=1,
        )
        selected_value_rows = jnp.concatenate(
            [
                jnp.take(cache_v, lists, axis=0).reshape(blocks_here, listed * BLOCK, DH),
                jnp.take(slab_v, slab_index, axis=0).reshape(blocks_here, WIN * BLOCK, DH),
            ],
            axis=1,
        )
        logit_matrix = (
            jnp.einsum(
                "yav,ycv->yac",
                query_tile_rows,
                selected_key_rows,
                preferred_element_type=jnp.float32,
            )
            * score_scale
        )
        probability_weights = softmax_weights(logit_matrix, full_mask)
        weighted_total = jnp.einsum(
            "fgx,fxc->fgc",
            probability_weights,
            selected_value_rows,
            preferred_element_type=jnp.float32,
        )
        return weighted_total.astype(jnp.bfloat16)

    pair_count = head_count // 2

    def attend_pair(item):
        pair_queries, pair_lists, pair_numbers = item
        return jax.vmap(attend)(pair_queries, pair_lists, pair_numbers)

    results = lax.map(
        attend_pair,
        (
            query_heads.reshape(pair_count, 2, blocks_here, BLOCK, DH),
            block_lists.reshape(pair_count, 2, blocks_here, listed),
            jnp.arange(head_count, dtype=jnp.int32).reshape(pair_count, 2),
        ),
    )
    results = results.reshape(head_count, blocks_here, BLOCK, DH).transpose(1, 2, 0, 3)
    results = results.reshape(blocks_here * BLOCK, head_count * DH)
    return lax.all_to_all(results, "head", split_axis=0, concat_axis=1, tiled=True)


def solution(mesh):
    return jax.shard_map(
        per_device,
        mesh=mesh,
        in_specs=(
            P(("seq", "head"), None),
            P("seq", "head"),
            P("seq", "head"),
            P("seq", "head"),
            P("seq", "head"),
            P("head", "seq", None),
        ),
        out_specs=P(("seq", "head"), None),
        check_vma=False,
    )
```

profile of v0, /device:TPU:32, one launch (start us, length us, event | category | flops | bytes accessed | tf_op | source)
XLA Modules:
  0.0 750.2 jit_solution(7762240975053461179)
XLA Ops:
  11.2 16.8 %all-to-all-start = ((bf16[32,8,1024]{2,0,1:T(8,128)(2,1)}), bf16[32,8,1024]{2,0,1:T(8,128)(2,1)S(1)}, u32[]{:S(2)}, u32[]{:S(2)}) async-start(bf16[32,8,1024]{2,0,1:T(8,128)(2,1)} %bitcast.61), calls=%async_computation | async-start | bytes 1048576 | tf_op jit(solution)/shard_map/all_to_all | solution.py:28
  29.6 35.1 %all-to-all-done = bf16[32,8,1024]{2,0,1:T(8,128)(2,1)S(1)} async-done(((bf16[32,8,1024]{2,0,1:T(8,128)(2,1)}), bf16[32,8,1024]{2,0,1:T(8,128)(2,1)S(1)}, u32[]{:S(2)}, u32[]{:S(2)}) %all-to-all-start) | async-done | bytes 524320 | tf_op jit(solution)/shard_map/all_to_all | solution.py:28
  65.6 79.8 %all-gather.5.cloned.1.call-done = bf16[4096,128]{1,0:T(8,128)(2,1)} async-done(((bf16[64,128]{1,0:T(8,128)(2,1)}), bf16[4096,128]{1,0:T(8,128)(2,1)}) %all-gather.5.cloned.1.call-update) | async-done | bytes 1048592 | tf_op jit(solution)/shard_map/all_gather | solution.py:29
  145.4 119.9 %all-gather.9.cloned.1.call-done = bf16[4096,128]{1,0:T(8,128)(2,1)} async-done(((bf16[64,128]{1,0:T(8,128)(2,1)}), bf16[4096,128]{1,0:T(8,128)(2,1)}) %all-gather.9.cloned.1.call-update) | async-done | bytes 1048592 | tf_op jit(solution)/shard_map/all_gather | solution.py:30
  265.3 121.0 %all-gather.7.cloned.1.call-done = bf16[16384,128]{1,0:T(8,128)(2,1)} async-done(((bf16[256,128]{1,0:T(8,128)(2,1)}), bf16[16384,128]{1,0:T(8,128)(2,1)}) %all-gather.7.cloned.1.call-update) | async-done | bytes 4194320 | tf_op jit(solution)/shard_map/all_gather | solution.py:31
  386.3 120.4 %all-gather.11.cloned.1.call-done = bf16[16384,128]{1,0:T(8,128)(2,1)} async-done(((bf16[256,128]{1,0:T(8,128)(2,1)}), bf16[16384,128]{1,0:T(8,128)(2,1)}) %all-gather.11.cloned.1.call-update) | async-done | bytes 4194320 | tf_op jit(solution)/shard_map/all_gather | solution.py:32
  506.7 188.8 %while.14 = (s32[]{:T(128)}, bf16[4,2,4,64,128]{4,3,2,1,0:T(8,128)(2,1)}, pred[4,64,1792]{2,1,0:T(8,128)(4,1)}, bf16[4,2,4,64,128]{4,1,0,3,2:T(2,128)(2,1)}, bf1...) while((s32[]{:T(128)}, ...), condition=%wide.region_3.6_spmd.clone.clone, body=%wide.region_0.5_spmd.clone.clone.sunk | while | flops 494608064 | bytes 110837584 | solution.py:100
  506.7 7.8 %broadcast.365 = bf16[2,256,64,128]{3,2,1,0:T(8,128)(2,1)} broadcast(bf16[256,64,128]{2,1,0:T(8,128)(2,1)} %bitcast.104), dimensions={1,2,3} | broadcast | bytes 12582912 | tf_op jit(solution)/shard_map/while/body/eval_jaxpr/vmap(jit(dynamic_index_in_dim))/squeeze | solution.py:60
  514.7 4.0 gather_fusion
  518.8 7.8 %broadcast.366 = bf16[2,256,64,128]{3,2,1,0:T(8,128)(2,1)} broadcast(bf16[256,64,128]{2,1,0:T(8,128)(2,1)} %bitcast.106), dimensions={1,2,3} | broadcast | bytes 12582912 | tf_op jit(solution)/shard_map/while/body/eval_jaxpr/vmap(jit(dynamic_index_in_dim))/squeeze | solution.py:61
  526.6 4.1 gather_fusion.1
  536.8 3.7 gather_fusion.3
  548.9 5.0 fusion.38
  553.9 7.8 %broadcast.365 = bf16[2,256,64,128]{3,2,1,0:T(8,128)(2,1)} broadcast(bf16[256,64,128]{2,1,0:T(8,128)(2,1)} %bitcast.104), dimensions={1,2,3} | broadcast | bytes 12582912 | tf_op jit(solution)/shard_map/while/body/eval_jaxpr/vmap(jit(dynamic_index_in_dim))/squeeze | solution.py:60
  561.8 4.0 gather_fusion
  566.0 7.8 %broadcast.366 = bf16[2,256,64,128]{3,2,1,0:T(8,128)(2,1)} broadcast(bf16[256,64,128]{2,1,0:T(8,128)(2,1)} %bitcast.106), dimensions={1,2,3} | broadcast | bytes 12582912 | tf_op jit(solution)/shard_map/while/body/eval_jaxpr/vmap(jit(dynamic_index_in_dim))/squeeze | solution.py:61
  573.8 4.1 gather_fusion.1
  584.0 3.7 gather_fusion.3
  596.1 5.0 fusion.38
  601.1 7.8 %broadcast.365 = bf16[2,256,64,128]{3,2,1,0:T(8,128)(2,1)} broadcast(bf16[256,64,128]{2,1,0:T(8,128)(2,1)} %bitcast.104), dimensions={1,2,3} | broadcast | bytes 12582912 | tf_op jit(solution)/shard_map/while/body/eval_jaxpr/vmap(jit(dynamic_index_in_dim))/squeeze | solution.py:60
  609.0 4.0 gather_fusion
  613.1 7.8 %broadcast.366 = bf16[2,256,64,128]{3,2,1,0:T(8,128)(2,1)} broadcast(bf16[256,64,128]{2,1,0:T(8,128)(2,1)} %bitcast.106), dimensions={1,2,3} | broadcast | bytes 12582912 | tf_op jit(solution)/shard_map/while/body/eval_jaxpr/vmap(jit(dynamic_index_in_dim))/squeeze | solution.py:61
  621.0 4.1 gather_fusion.1
  631.2 3.7 gather_fusion.3
  643.3 5.0 fusion.38
  648.2 7.8 %broadcast.365 = bf16[2,256,64,128]{3,2,1,0:T(8,128)(2,1)} broadcast(bf16[256,64,128]{2,1,0:T(8,128)(2,1)} %bitcast.104), dimensions={1,2,3} | broadcast | bytes 12582912 | tf_op jit(solution)/shard_map/while/body/eval_jaxpr/vmap(jit(dynamic_index_in_dim))/squeeze | solution.py:60
  656.2 4.0 gather_fusion
  660.3 7.8 %broadcast.366 = bf16[2,256,64,128]{3,2,1,0:T(8,128)(2,1)} broadcast(bf16[256,64,128]{2,1,0:T(8,128)(2,1)} %bitcast.106), dimensions={1,2,3} | broadcast | bytes 12582912 | tf_op jit(solution)/shard_map/while/body/eval_jaxpr/vmap(jit(dynamic_index_in_dim))/squeeze | solution.py:61
  668.1 4.1 gather_fusion.1
  678.4 3.7 gather_fusion.3
  690.4 5.0 fusion.38
  697.0 45.8 %all_to_all.35 = bf16[8,32,1024]{2,1,0:T(8,128)(2,1)S(1)} all-to-all(bf16[8,32,1024]{2,1,0:T(8,128)(2,1)S(1)} %all_to_all.29), channel_id=1, replica_groups=mesh['seq'=64,'head'=8] {'head'}, dimensions={0} | all-to-all | bytes 1048576 | tf_op jit(solution)/shard_map/all_to_all | solution.py:110
  (129 shorter events, 68.2 us)
Async XLA Ops:
  6.5 500.1 %copy-start.5 = (s32[8,4,24]{2,1,0:T(4,128)S(1)}, s32[8,4,24]{2,1,0:T(4,128)}, u32[]{:S(2)}) copy-start(s32[8,4,24]{2,1,0:T(4,128)} %param.17) | copy-start | bytes 9220
  6.5 138.8 %all-gather.5.cloned.1.call-start = ((), (), s32[]{:S(2)}) async-start(), calls=%async_computation.2 | async-start | bytes 1064960 | tf_op jit(solution)/shard_map/all_gather | solution.py:29
  7.3 258.0 %all-gather.9.cloned.1.call-start = ((), (), s32[]{:S(2)}) async-start(), calls=%async_computation.4 | async-start | bytes 1064960 | tf_op jit(solution)/shard_map/all_gather | solution.py:30
  8.0 378.3 %all-gather.7.cloned.1.call-start = ((), (), s32[]{:S(2)}) async-start(), calls=%async_computation.3 | async-start | bytes 4259840 | tf_op jit(solution)/shard_map/all_gather | solution.py:31
  8.7 497.9 %all-gather.11.cloned.1.call-start = ((), (), s32[]{:S(2)}) async-start(), calls=%async_computation.5 | async-start | bytes 4259840 | tf_op jit(solution)/shard_map/all_gather | solution.py:32
  11.2 53.5 %all-to-all-start = ((bf16[32,8,1024]{2,0,1:T(8,128)(2,1)}), bf16[32,8,1024]{2,0,1:T(8,128)(2,1)S(1)}, u32[]{:S(2)}, u32[]{:S(2)}) async-start(bf16[32,8,1024]{2,0,1:T(8,128)(2,1)} %bitcast.61), calls=%async_computation | async-start | bytes 1048576 | tf_op jit(solution)/shard_map/all_to_all | solution.py:28
  526.6 5.3 copy-start.1
  532.5 3.7 copy-start.2
  540.5 4.3 copy-start.3
  540.5 4.3 copy-start.4
  546.3 1.8 copy-start
  573.8 5.3 copy-start.1
  579.7 3.7 copy-start.2
  587.6 4.3 copy-start.3
  587.6 4.3 copy-start.4
  593.5 1.8 copy-start
  621.0 5.3 copy-start.1
  626.8 3.7 copy-start.2
  634.8 4.3 copy-start.3
  634.8 4.3 copy-start.4
  640.7 1.8 copy-start
  668.1 5.3 copy-start.1
  674.0 3.7 copy-start.2
  682.0 4.3 copy-start.3
  682.0 4.3 copy-start.4
  687.9 1.8 copy-start
Sparse Core Ops, SparseCore 0:
  9.5 135.8 all-gather.4
  147.5 117.7 all-gather.8
  267.5 118.7 all-gather.6
  388.3 118.3 all-gather.10
where the time goes:
time: 751 us; the launch traced here: 750 us
  waiting for transfers between devices  479 us (64%)
  local copies, waits for them, and re-layouts  147 us (20%)
  blocking collectives  45.8 us (6%)
  matrix products  26.2 us (3%)
  other arithmetic  21.6 us (3%)
  starting transfers between devices  16.9 us (2%)
  between operations  13.2 us (2%)
    all_gather x1, waiting for transfers between devices, per_device(): source_keys = lax.all_gather(slab_keys, 'seq', axis=0, tiled=True)  121 us
    all_gather x1, waiting for transfers between devices, per_device(): source_values = lax.all_gather(slab_values, 'seq', axis=0, tiled=True)  120 us
    all_gather x1, waiting for transfers between devices, per_device(): gathered_values = lax.all_gather(cache_values, 'seq', axis=0, tiled=True)  120 us
    all_gather x1, waiting for transfers between devices, per_device(): gathered_keys = lax.all_gather(cache_keys, 'seq', axis=0, tiled=True)  79.8 us
    all_to_all x1, blocking collectives, per_device(): lax.all_to_all(results, 'head', split_axis=0, concat_axis=1, tiled=True)  45.8 us
    all_to_all x1, waiting for transfers between devices, per_device(): lax.all_to_all(queries, 'head', split_axis=1, concat_axis=0, tiled=True)  35.1 us
    squeeze x4, local copies, waits for them, and re-layouts, attend(): lax.dynamic_index_in_dim(slab_value_blocks, kv_number, 0, keepdims=False)  31.3 us
    squeeze x4, local copies, waits for them, and re-layouts, attend(): lax.dynamic_index_in_dim(slab_key_blocks, kv_number, 0, keepdims=False)  31.3 us
  transfers between devices with their start and end apart: 5, of which 5 were waited for; matrix products, arithmetic and copies ran while one was open for 1% of the time, Pallas kernels for 0%

commit v1 on v0

--- a/solution.py
+++ b/solution.py
@@ -27,7 +27,15 @@
     slab_valid = query_blocks[:, None] - offsets[None, :] >= 0
     arrived = lax.all_to_all(queries, "head", split_axis=1, concat_axis=0, tiled=True)
     gathered_keys = lax.all_gather(cache_keys, "seq", axis=0, tiled=True)
-    gathered_values = lax.all_gather(cache_values, "seq", axis=0, tiled=True)
+
+    def fit_pipes_on(t0):
+        current_arr = tuple((t0 for _ in range(lax.axis_size("seq"))))
+        outcome_arr = jnp.stack(current_arr, 0)
+        return jnp.concatenate(
+            lax.all_to_all(outcome_arr, axis_name="seq", split_axis=0, concat_axis=0), 0
+        )
+
+    gathered_values = fit_pipes_on(cache_values)
     source_keys = lax.all_gather(slab_keys, "seq", axis=0, tiled=True)
     source_values = lax.all_gather(slab_values, "seq", axis=0, tiled=True)
     fetch_slab_index = jnp.maximum(query_blocks[:, None] - offsets[None, :], 0)

time: 751 us -> 648 us (0.86)
  waiting for transfers between devices: 479 us -> 325 us
  blocking collectives: 45.8 us -> 99 us
  starting transfers between devices: 16.9 us -> 8.44 us
    all_gather x1 -> x0, waiting for transfers between devices: 120 us -> none  [per_device(): gathered_values = lax.all_gather(cache_values, 'seq', axis=0, tiled=True)]
    all_to_all x0 -> x1, blocking collectives: none -> 53.2 us  [per_device(): lax.all_to_all(queries, 'head', split_axis=1, concat_axis=0, tiled=True)]
    all_to_all x1, waiting for transfers between devices: 35.1 us -> 0.01 us  [fit_pipes_on(): lax.all_to_all(outcome_arr, axis_name='seq', split_axis=0, concat_axis=0)]
    all_to_all x1, starting transfers between devices: 16.8 us -> 8.36 us  [fit_pipes_on(): lax.all_to_all(outcome_arr, axis_name='seq', split_axis=0, concat_axis=0)]
  transfers between devices with their start and end apart: 5 -> 4, of which waited for: 5 -> 3; matrix products, arithmetic and copies ran while one was open for 1% -> 1% of each run, Pallas kernels for 0% -> 0%
where the time goes in v1:
time: 648 us; the launch traced here: 647 us
  waiting for transfers between devices  325 us (50%)
  local copies, waits for them, and re-layouts  153 us (24%)
  blocking collectives  99 us (15%)
  matrix products  26.2 us (4%)
  other arithmetic  21.7 us (3%)
  between operations  13.2 us (2%)
  starting transfers between devices  8.44 us (1%)
    all_gather x1, waiting for transfers between devices, per_device(): source_keys = lax.all_gather(slab_keys, 'seq', axis=0, tiled=True)  127 us
    all_gather x1, waiting for transfers between devices, per_device(): source_values = lax.all_gather(slab_values, 'seq', axis=0, tiled=True)  121 us
    all_gather x1, waiting for transfers between devices, per_device(): gathered_keys = lax.all_gather(cache_keys, 'seq', axis=0, tiled=True)  74.8 us
    all_to_all x1, blocking collectives, per_device(): lax.all_to_all(queries, 'head', split_axis=1, concat_axis=0, tiled=True)  53.2 us
    all_to_all x1, blocking collectives, per_device(): lax.all_to_all(results, 'head', split_axis=0, concat_axis=1, tiled=True)  45.8 us
    squeeze x4, local copies, waits for them, and re-layouts, attend(): lax.dynamic_index_in_dim(slab_value_blocks, kv_number, 0, keepdims=False)  31.3 us
    squeeze x4, local copies, waits for them, and re-layouts, attend(): lax.dynamic_index_in_dim(slab_key_blocks, kv_number, 0, keepdims=False)  31.3 us
    dot_general x4, matrix products, attend(): jnp.einsum('fgx,fxc->fgc', probability_weights, selected_value_rows, pref...  19.9 us
  transfers between devices with their start and end apart: 4, of which 3 were waited for; matrix products, arithmetic and copies ran while one was open for 1% of the time, Pallas kernels for 0%

profile of v1, /device:TPU:32, one launch (start us, length us, event | category | flops | bytes accessed | tf_op | source)
XLA Modules:
  0.0 646.8 jit_solution(6135728305005097109)
XLA Ops:
  9.8 53.2 %all_to_all.40 = bf16[32,8,1024]{2,0,1:T(8,128)(2,1)S(1)} all-to-all(bf16[32,8,1024]{2,0,1:T(8,128)(2,1)S(1)} %bitcast.119), channel_id=1, replica_groups=mesh['seq'=64,'head'=8] {'head'}, dimensions={1} | all-to-all | bytes 1048576 | tf_op jit(solution)/shard_map/all_to_all | solution.py:28
  65.0 8.4 %all-to-all-start.1 = ((bf16[64,64,128]{2,1,0:T(8,128)(2,1)}), bf16[64,64,128]{2,1,0:T(8,128)(2,1)}, u32[]{:S(2)}, u32[]{:S(2)}) async-start(bf16[64,64,128]{2,1,0:T(8,128)(2,1)} %stack.2), calls=%async_computation.1 | async-start | bytes 2097152 | tf_op jit(solution)/shard_map/all_to_all | solution.py:35
  75.8 74.8 %all-gather.4.cloned.1.call-done = bf16[4096,128]{1,0:T(8,128)(2,1)} async-done(((bf16[64,128]{1,0:T(8,128)(2,1)}), bf16[4096,128]{1,0:T(8,128)(2,1)}) %all-gather.4.cloned.1.call-update) | async-done | bytes 1048592 | tf_op jit(solution)/shard_map/all_gather | solution.py:29
  150.7 127.3 %all-gather.6.cloned.1.call-done = bf16[16384,128]{1,0:T(8,128)(2,1)} async-done(((bf16[256,128]{1,0:T(8,128)(2,1)}), bf16[16384,128]{1,0:T(8,128)(2,1)}) %all-gather.6.cloned.1.call-update) | async-done | bytes 4194320 | tf_op jit(solution)/shard_map/all_gather | solution.py:39
  278.0 120.6 %all-gather.8.cloned.1.call-done = bf16[16384,128]{1,0:T(8,128)(2,1)} async-done(((bf16[256,128]{1,0:T(8,128)(2,1)}), bf16[16384,128]{1,0:T(8,128)(2,1)}) %all-gather.8.cloned.1.call-update) | async-done | bytes 4194320 | tf_op jit(solution)/shard_map/all_gather | solution.py:40
  398.5 193.5 %while.14 = (s32[]{:T(128)}, bf16[4,2,4,64,128]{4,3,2,1,0:T(8,128)(2,1)}, pred[4,64,1792]{2,1,0:T(8,128)(4,1)}, bf16[4,2,4,64,128]{4,1,0,3,2:T(2,128)(2,1)}, bf1...) while((s32[]{:T(128)}, ...), condition=%wide.region_3.6_spmd.clone.clone, body=%wide.region_0.5_spmd.clone.clone.sunk | while | flops 494608064 | bytes 106643248 | solution.py:108
  398.5 7.8 %broadcast.367 = bf16[2,256,64,128]{3,2,1,0:T(8,128)(2,1)} broadcast(bf16[256,64,128]{2,1,0:T(8,128)(2,1)} %bitcast.104), dimensions={1,2,3} | broadcast | bytes 12582912 | tf_op jit(solution)/shard_map/while/body/eval_jaxpr/vmap(jit(dynamic_index_in_dim))/squeeze | solution.py:68
  406.5 4.0 gather_fusion
  410.6 7.8 %broadcast.368 = bf16[2,256,64,128]{3,2,1,0:T(8,128)(2,1)} broadcast(bf16[256,64,128]{2,1,0:T(8,128)(2,1)} %bitcast.106), dimensions={1,2,3} | broadcast | bytes 12582912 | tf_op jit(solution)/shard_map/while/body/eval_jaxpr/vmap(jit(dynamic_index_in_dim))/squeeze | solution.py:69
  418.5 4.1 gather_fusion.1
  424.5 3.6 gather_fusion.2
  429.8 3.7 gather_fusion.3
  441.9 5.0 fusion.38
  446.9 7.8 %broadcast.367 = bf16[2,256,64,128]{3,2,1,0:T(8,128)(2,1)} broadcast(bf16[256,64,128]{2,1,0:T(8,128)(2,1)} %bitcast.104), dimensions={1,2,3} | broadcast | bytes 12582912 | tf_op jit(solution)/shard_map/while/body/eval_jaxpr/vmap(jit(dynamic_index_in_dim))/squeeze | solution.py:68
  454.9 4.0 gather_fusion
  459.0 7.8 %broadcast.368 = bf16[2,256,64,128]{3,2,1,0:T(8,128)(2,1)} broadcast(bf16[256,64,128]{2,1,0:T(8,128)(2,1)} %bitcast.106), dimensions={1,2,3} | broadcast | bytes 12582912 | tf_op jit(solution)/shard_map/while/body/eval_jaxpr/vmap(jit(dynamic_index_in_dim))/squeeze | solution.py:69
  466.8 4.1 gather_fusion.1
  478.2 3.7 gather_fusion.3
  490.3 5.0 fusion.38
  495.3 7.8 %broadcast.367 = bf16[2,256,64,128]{3,2,1,0:T(8,128)(2,1)} broadcast(bf16[256,64,128]{2,1,0:T(8,128)(2,1)} %bitcast.104), dimensions={1,2,3} | broadcast | bytes 12582912 | tf_op jit(solution)/shard_map/while/body/eval_jaxpr/vmap(jit(dynamic_index_in_dim))/squeeze | solution.py:68
  503.3 4.0 gather_fusion
  507.4 7.8 %broadcast.368 = bf16[2,256,64,128]{3,2,1,0:T(8,128)(2,1)} broadcast(bf16[256,64,128]{2,1,0:T(8,128)(2,1)} %bitcast.106), dimensions={1,2,3} | broadcast | bytes 12582912 | tf_op jit(solution)/shard_map/while/body/eval_jaxpr/vmap(jit(dynamic_index_in_dim))/squeeze | solution.py:69
  515.2 4.1 gather_fusion.1
  526.6 3.7 gather_fusion.3
  538.7 5.0 fusion.38
  543.7 7.8 %broadcast.367 = bf16[2,256,64,128]{3,2,1,0:T(8,128)(2,1)} broadcast(bf16[256,64,128]{2,1,0:T(8,128)(2,1)} %bitcast.104), dimensions={1,2,3} | broadcast | bytes 12582912 | tf_op jit(solution)/shard_map/while/body/eval_jaxpr/vmap(jit(dynamic_index_in_dim))/squeeze | solution.py:68
  551.7 4.0 gather_fusion
  555.8 7.8 %broadcast.368 = bf16[2,256,64,128]{3,2,1,0:T(8,128)(2,1)} broadcast(bf16[256,64,128]{2,1,0:T(8,128)(2,1)} %bitcast.106), dimensions={1,2,3} | broadcast | bytes 12582912 | tf_op jit(solution)/shard_map/while/body/eval_jaxpr/vmap(jit(dynamic_index_in_dim))/squeeze | solution.py:69
  563.6 4.1 gather_fusion.1
  575.0 3.7 gather_fusion.3
  587.1 5.0 fusion.38
  593.7 45.8 %all_to_all.41 = bf16[8,32,1024]{2,1,0:T(8,128)(2,1)S(1)} all-to-all(bf16[8,32,1024]{2,1,0:T(8,128)(2,1)S(1)} %all_to_all.33), channel_id=1, replica_groups=mesh['seq'=64,'head'=8] {'head'}, dimensions={0} | all-to-all | bytes 1048576 | tf_op jit(solution)/shard_map/all_to_all | solution.py:118
  (120 shorter events, 69.9 us)
Async XLA Ops:
  6.5 392.0 %copy-start.4 = (s32[8,4,24]{2,1,0:T(4,128)S(1)}, s32[8,4,24]{2,1,0:T(4,128)}, u32[]{:S(2)}) copy-start(s32[8,4,24]{2,1,0:T(4,128)} %param.17) | copy-start | bytes 9220
  6.5 144.1 %all-gather.4.cloned.1.call-start = ((), (), s32[]{:S(2)}) async-start(), calls=%async_computation.3 | async-start | bytes 1064960 | tf_op jit(solution)/shard_map/all_gather | solution.py:29
  7.3 270.7 %all-gather.6.cloned.1.call-start = ((), (), s32[]{:S(2)}) async-start(), calls=%async_computation.4 | async-start | bytes 4259840 | tf_op jit(solution)/shard_map/all_gather | solution.py:39
  8.0 390.5 %all-gather.8.cloned.1.call-start = ((), (), s32[]{:S(2)}) async-start(), calls=%async_computation.5 | async-start | bytes 4259840 | tf_op jit(solution)/shard_map/all_gather | solution.py:40
  65.0 85.7 %all-to-all-start.1 = ((bf16[64,64,128]{2,1,0:T(8,128)(2,1)}), bf16[64,64,128]{2,1,0:T(8,128)(2,1)}, u32[]{:S(2)}, u32[]{:S(2)}) async-start(bf16[64,64,128]{2,1,0:T(8,128)(2,1)} %stack.2), calls=%async_computation.1 | async-start | bytes 2097152 | tf_op jit(solution)/shard_map/all_to_all | solution.py:35
  418.4 5.3 copy-start.1
  433.5 4.3 copy-start.2
  433.5 4.3 copy-start.3
  439.4 1.8 copy-start
  466.8 5.3 copy-start.1
  481.9 4.3 copy-start.2
  481.9 4.3 copy-start.3
  487.8 1.8 copy-start
  515.2 5.3 copy-start.1
  530.3 4.3 copy-start.2
  530.3 4.3 copy-start.3
  536.1 1.8 copy-start
  563.6 5.3 copy-start.1
  578.6 4.3 copy-start.2
  578.6 4.3 copy-start.3
  584.5 1.8 copy-start
Sparse Core Ops, SparseCore 0:
  9.5 141.1 all-gather.3
  152.8 125.0 all-gather.5
  280.1 118.3 all-gather.7
